TPU v7x, 128 devices: a whole 4x4x4 slice. The times are simulated.
128 devices in a mesh: patch: 16 (over z, x), exp: 8 (over y, core).
Axes of the slice: x: 4, y: 4, z: 4, core: 2. Of those that a mesh axis runs over, the one named last changes fastest.
Arguments:
- sky_model: float32 [16, 8, 6, 256, 256], P('patch', 'exp'), may hold values from -6 to 6
- stamp_pixels: bfloat16 [16384, 256, 256], P(('patch', 'exp')), may hold values from -6 to 6
- stamp_patch: int32 [16384, 1], P(('patch', 'exp')), may hold values from 0 to 15; in each aligned block of 128 rows (0 to 127, 128 to 255, ...) at most 12 rows name the same one
- stamp_band: int32 [16384], P(('patch', 'exp')), may hold values from 0 to 5
- psf_taps: bfloat16 [16384, 2, 21], P(('patch', 'exp')), may hold values from 0.019897461 to 0.19921875
- stamp_gain: bfloat16 [16384], P(('patch', 'exp')), may hold values from 0.5 to 2
- stamp_weight: bfloat16 [16384], P(('patch', 'exp')), may hold values from 0.25 to 4
Outputs:
- new_model: float32 [16, 8, 6, 256, 256], P('patch', 'exp')
- step_rms: float32 [], replicated
Inputs may be any that keep to these rules, and one draw needn't show every extreme that they name: `stamp_patch`: among the stamps of one device no patch is named by more than 12 stamps, a bound that some block reaches.
All inputs are finite; a program needn't handle non-finite values.
Results may differ from a plain program's by a relative error of at most 0.013.
Values may be sent and summed in bfloat16 or wider, within the bound.
A program may use at most 192 MiB of HBM per device.

v0:
```python
import jax
import jax.numpy as jnp
from jax import lax
from jax.sharding import PartitionSpec as P

step_rate = 0.2


def banded_matrices(tap_values, tile_size):
    tap_length = tap_values.shape[-1]
    half_width = (tap_length - 1) // 2
    pixel_index = jnp.arange(tile_size, dtype=jnp.int32)
    offset = pixel_index[None, :] - pixel_index[:, None] + half_width
    tap_table = (
        offset[None, :, :] == jnp.arange(tap_length, dtype=jnp.int32)[:, None, None]
    ).astype(jnp.bfloat16)
    return jnp.einsum(
        "sk,kij->sij", tap_values, tap_table, preferred_element_type=jnp.float32
    ).astype(jnp.bfloat16)


def stamp_adjoint(tile_sel, pixels, tap_values, gain_rows, weight_rows):
    tile_size = pixels.shape[-1]
    row_kernel = banded_matrices(tap_values[:, 0], tile_size)
    col_kernel = banded_matrices(tap_values[:, 1], tile_size)
    blurred = jnp.einsum(
        "sab,scb->sac", tile_sel, col_kernel, preferred_element_type=jnp.float32
    ).astype(jnp.bfloat16)
    gain_wide = gain_rows.astype(jnp.float32)[:, None, None]
    predicted = gain_wide * jnp.einsum(
        "sab,sbc->sac", row_kernel, blurred, preferred_element_type=jnp.float32
    )
    residual = (
        weight_rows.astype(jnp.float32)[:, None, None] * (predicted - pixels.astype(jnp.float32))
    ).astype(jnp.bfloat16)
    backward = jnp.einsum(
        "sba,sbc->sac", row_kernel, residual, preferred_element_type=jnp.float32
    ).astype(jnp.bfloat16)
    return gain_wide * jnp.einsum(
        "sab,sbc->sac", backward, col_kernel, preferred_element_type=jnp.float32
    )


def per_device(
    sky_model, stamp_pixels, stamp_patch, stamp_band, psf_taps, stamp_gain, stamp_weight
):
    band_count = sky_model.shape[2]
    tile_size = sky_model.shape[-1]
    stamp_count = stamp_pixels.shape[0]
    tap_length = psf_taps.shape[-1]
    block_rows = 32
    model_half = sky_model.astype(jnp.bfloat16)
    patches = lax.axis_size("patch")
    gathered = lax.all_gather(model_half, "patch", axis=0, tiled=True)
    key_count = gathered.shape[0] * band_count
    flat_tiles = gathered.reshape(key_count, tile_size, tile_size)
    tile_keys = stamp_patch[:, 0] * band_count + stamp_band
    block_count = stamp_count // block_rows
    block_inputs = (
        stamp_pixels.reshape(block_count, block_rows, tile_size, tile_size),
        tile_keys.reshape(block_count, block_rows),
        psf_taps.reshape(block_count, block_rows, 2, tap_length),
        stamp_gain.reshape(block_count, block_rows),
        stamp_weight.reshape(block_count, block_rows),
    )

    def source_block(running, block_parts):
        pixels, keys_block, tap_values, gain_rows, weight_rows = block_parts
        tile_sel = jnp.take(flat_tiles, keys_block, axis=0)
        adjoint = stamp_adjoint(tile_sel, pixels, tap_values, gain_rows, weight_rows)
        return (running.at[keys_block].add(adjoint), None)

    result = lax.scan(
        source_block, jnp.zeros((key_count, tile_size, tile_size), jnp.float32), block_inputs
    )
    gradient = lax.psum_scatter(
        result[0].reshape(gathered.shape).astype(jnp.bfloat16),
        "patch",
        scatter_dimension=0,
        tiled=True,
    ).astype(jnp.float32)
    step_field = step_rate * gradient
    new_model = sky_model - step_field
    square_sum = lax.psum(jnp.sum(step_field * step_field), ("patch", "exp"))
    entry_count = patches * lax.axis_size("exp") * band_count * tile_size * tile_size
    step_rms = jnp.sqrt(square_sum / entry_count + 1e-06)
    return (new_model, step_rms)


def solution(mesh):
    return jax.shard_map(
        per_device,
        mesh=mesh,
        in_specs=(
            P("patch", "exp", None, None, None),
            P(("patch", "exp"), None, None),
            P(("patch", "exp"), None),
            P(("patch", "exp")),
            P(("patch", "exp"), None, None),
            P(("patch", "exp")),
            P(("patch", "exp")),
        ),
        out_specs=(P("patch", "exp", None, None, None), P()),
        check_vma=False,
    )
```

profile of v0, /device:TPU:1, one launch (start us, length us, event | category | flops | bytes accessed | tf_op | source)
XLA Modules:
  0.0 557.4 jit_solution(9071368639380420495)
XLA Ops:
  12.7 91.4 %all-gather.2.cloned.1.call-done = bf16[16,1,6,256,256]{4,3,2,1,0:T(8,128)(2,1)} async-done(((bf16[1,1,6,256,256]{4,3,2,1,0:T(8,128)(2,1)}), bf16[16,1,6,256,256]{4,3,2,1,0:T(8,128)(2,1)}) %all-gather.2.cloned.1.call-update) | async-done | bytes 12582928 | tf_op jit(solution)/shard_map/all_gather | solution.py:54
  104.1 11.4 %broadcast_in_dim.12 = f32[96,256,256]{2,1,0:T(8,128)} broadcast(f32[]{:T(128)} %constant.24.clone.1), dimensions={} | broadcast | bytes 25165828 | tf_op jit(solution)/shard_map/broadcast_in_dim | solution.py:74
  115.5 258.0 %while.10 = (s32[]{:T(128)}, f32[96,256,256]{2,1,0:T(8,128)}, s32[4,32]{1,0:T(4,128)S(1)}, bf16[4,32]{1,0:T(4,128)(2,1)S(1)}, bf16[4,32,2,21]{1,3,2,0:T(8,128)(2...) while((s32[]{:T(128)}, f32[96,256,256]{2,1,0:T(8,128)}, ...), condition=%wide.region_2.3_spmd, body=%wide.region_0.2_spmd.sunk | while | flops 4494984704 | bytes 135027696 | solution.py:73
  115.6 7.3 %gather_fusion = bf16[32,256,256]{2,1,0:T(8,128)(2,1)} fusion(bf16[96,256,256]{2,1,0:T(8,128)(2,1)} %get-tuple-element.158, s32[1024]{0:T(1024)S(1)} %pad_clamp_fusion.2), kind=kCustom, calls=%fused_computation.clone.1 | custom fusion | bytes 8388736 | tf_op jit(solution)/shard_map/while/body/eval_jaxpr/jit(_take)/gather | solution.py:69
  125.2 5.0 fusion.70
  130.2 3.3 fusion.69
  133.5 7.5 %copy.28 = bf16[32,256,256]{1,2,0:T(8,128)(2,1)} copy(bf16[32,256,256]{2,0,1:T(8,128)(2,1)} %fusion.69) | data formatting | bytes 8388608 | tf_op jit(solution)/shard_map/while/body/eval_jaxpr/convert_element_type | solution.py:19
  141.0 10.6 %fusion.71 = bf16[32,256,256]{2,1,0:T(8,128)(2,1)} fusion(bf16[32,256,256]{1,2,0:T(8,128)(2,1)} %copy.28, bf16[4,32,256,256]{3,2,1,0:T(8,128)(2,1)} %get-tuple-element.159, s32[]{:T(128)S(6)} %copy.32, f32[32]{0:T(128)S(1)} %get-tuple-element.133, f32[32]{0:T(128)S(1)} %get-tuple-element.132, bf16[32,256,256]{2,1,0:T(8,128)(2,1)} %fusion.70), kind=kOutput, calls=%fused_computation.8.clone.1 | convolution fusion | flops 2157969408 | bytes 20971780 | tf_op jit(solution)/shard_map/while/body/eval_jaxpr/sba,sbc->sac/dot_general | solution.py:36
  151.7 9.6 %broadcast_multiply_fusion.2 = f32[32,256,256]{2,1,0:T(8,128)} fusion(f32[32]{0:T(128)S(1)} %get-tuple-element.132, bf16[32,256,256]{2,0,1:T(8,128)(2,1)} %copy-done, bf16[32,256,256]{2,1,0:T(8,128)(2,1)} %fusion.71), kind=kOutput, calls=%fused_computation.18.clone.1 | convolution fusion | flops 1075838976 | bytes 16777344 | tf_op jit(solution)/shard_map/while/body/eval_jaxpr/sab,sbc->sac/dot_general | solution.py:39
  161.2 18.8 %scatter_fusion = f32[96,256,256]{2,1,0:T(8,128)} fusion(f32[96,256,256]{2,1,0:T(8,128)} %get-tuple-element.144, s32[32]{0:T(128)S(1)} %fusion.66, f32[32,256,256]{2,1,0:T(8,128)} %broadcast_multiply_fusion.2), kind=kCustom, calls=%fused_computation.1.clone.1 | custom fusion | flops 2097152 | bytes 25165952 | tf_op jit(solution)/shard_map/while/body/eval_jaxpr/scatter-add | solution.py:71
  180.1 7.3 %gather_fusion = bf16[32,256,256]{2,1,0:T(8,128)(2,1)} fusion(bf16[96,256,256]{2,1,0:T(8,128)(2,1)} %get-tuple-element.158, s32[1024]{0:T(1024)S(1)} %pad_clamp_fusion.2), kind=kCustom, calls=%fused_computation.clone.1 | custom fusion | bytes 8388736 | tf_op jit(solution)/shard_map/while/body/eval_jaxpr/jit(_take)/gather | solution.py:69
  189.7 5.0 fusion.70
  198.0 7.5 %copy.28 = bf16[32,256,256]{1,2,0:T(8,128)(2,1)} copy(bf16[32,256,256]{2,0,1:T(8,128)(2,1)} %fusion.69) | data formatting | bytes 8388608 | tf_op jit(solution)/shard_map/while/body/eval_jaxpr/convert_element_type | solution.py:19
  205.5 10.6 %fusion.71 = bf16[32,256,256]{2,1,0:T(8,128)(2,1)} fusion(bf16[32,256,256]{1,2,0:T(8,128)(2,1)} %copy.28, bf16[4,32,256,256]{3,2,1,0:T(8,128)(2,1)} %get-tuple-element.159, s32[]{:T(128)S(6)} %copy.32, f32[32]{0:T(128)S(1)} %get-tuple-element.133, f32[32]{0:T(128)S(1)} %get-tuple-element.132, bf16[32,256,256]{2,1,0:T(8,128)(2,1)} %fusion.70), kind=kOutput, calls=%fused_computation.8.clone.1 | convolution fusion | flops 2157969408 | bytes 20971780 | tf_op jit(solution)/shard_map/while/body/eval_jaxpr/sba,sbc->sac/dot_general | solution.py:36
  216.1 9.6 %broadcast_multiply_fusion.2 = f32[32,256,256]{2,1,0:T(8,128)} fusion(f32[32]{0:T(128)S(1)} %get-tuple-element.132, bf16[32,256,256]{2,0,1:T(8,128)(2,1)} %copy-done, bf16[32,256,256]{2,1,0:T(8,128)(2,1)} %fusion.71), kind=kOutput, calls=%fused_computation.18.clone.1 | convolution fusion | flops 1075838976 | bytes 16777344 | tf_op jit(solution)/shard_map/while/body/eval_jaxpr/sab,sbc->sac/dot_general | solution.py:39
  225.7 18.9 %scatter_fusion = f32[96,256,256]{2,1,0:T(8,128)} fusion(f32[96,256,256]{2,1,0:T(8,128)} %get-tuple-element.144, s32[32]{0:T(128)S(1)} %fusion.66, f32[32,256,256]{2,1,0:T(8,128)} %broadcast_multiply_fusion.2), kind=kCustom, calls=%fused_computation.1.clone.1 | custom fusion | flops 2097152 | bytes 25165952 | tf_op jit(solution)/shard_map/while/body/eval_jaxpr/scatter-add | solution.py:71
  244.7 7.3 %gather_fusion = bf16[32,256,256]{2,1,0:T(8,128)(2,1)} fusion(bf16[96,256,256]{2,1,0:T(8,128)(2,1)} %get-tuple-element.158, s32[1024]{0:T(1024)S(1)} %pad_clamp_fusion.2), kind=kCustom, calls=%fused_computation.clone.1 | custom fusion | bytes 8388736 | tf_op jit(solution)/shard_map/while/body/eval_jaxpr/jit(_take)/gather | solution.py:69
  254.2 5.0 fusion.70
  262.5 7.5 %copy.28 = bf16[32,256,256]{1,2,0:T(8,128)(2,1)} copy(bf16[32,256,256]{2,0,1:T(8,128)(2,1)} %fusion.69) | data formatting | bytes 8388608 | tf_op jit(solution)/shard_map/while/body/eval_jaxpr/convert_element_type | solution.py:19
  270.0 10.6 %fusion.71 = bf16[32,256,256]{2,1,0:T(8,128)(2,1)} fusion(bf16[32,256,256]{1,2,0:T(8,128)(2,1)} %copy.28, bf16[4,32,256,256]{3,2,1,0:T(8,128)(2,1)} %get-tuple-element.159, s32[]{:T(128)S(6)} %copy.32, f32[32]{0:T(128)S(1)} %get-tuple-element.133, f32[32]{0:T(128)S(1)} %get-tuple-element.132, bf16[32,256,256]{2,1,0:T(8,128)(2,1)} %fusion.70), kind=kOutput, calls=%fused_computation.8.clone.1 | convolution fusion | flops 2157969408 | bytes 20971780 | tf_op jit(solution)/shard_map/while/body/eval_jaxpr/sba,sbc->sac/dot_general | solution.py:36
  280.7 9.6 %broadcast_multiply_fusion.2 = f32[32,256,256]{2,1,0:T(8,128)} fusion(f32[32]{0:T(128)S(1)} %get-tuple-element.132, bf16[32,256,256]{2,0,1:T(8,128)(2,1)} %copy-done, bf16[32,256,256]{2,1,0:T(8,128)(2,1)} %fusion.71), kind=kOutput, calls=%fused_computation.18.clone.1 | convolution fusion | flops 1075838976 | bytes 16777344 | tf_op jit(solution)/shard_map/while/body/eval_jaxpr/sab,sbc->sac/dot_general | solution.py:39
  290.2 18.8 %scatter_fusion = f32[96,256,256]{2,1,0:T(8,128)} fusion(f32[96,256,256]{2,1,0:T(8,128)} %get-tuple-element.144, s32[32]{0:T(128)S(1)} %fusion.66, f32[32,256,256]{2,1,0:T(8,128)} %broadcast_multiply_fusion.2), kind=kCustom, calls=%fused_computation.1.clone.1 | custom fusion | flops 2097152 | bytes 25165952 | tf_op jit(solution)/shard_map/while/body/eval_jaxpr/scatter-add | solution.py:71
  309.1 7.3 %gather_fusion = bf16[32,256,256]{2,1,0:T(8,128)(2,1)} fusion(bf16[96,256,256]{2,1,0:T(8,128)(2,1)} %get-tuple-element.158, s32[1024]{0:T(1024)S(1)} %pad_clamp_fusion.2), kind=kCustom, calls=%fused_computation.clone.1 | custom fusion | bytes 8388736 | tf_op jit(solution)/shard_map/while/body/eval_jaxpr/jit(_take)/gather | solution.py:69
  318.7 5.0 fusion.70
  323.6 3.3 fusion.69
  327.0 7.5 %copy.28 = bf16[32,256,256]{1,2,0:T(8,128)(2,1)} copy(bf16[32,256,256]{2,0,1:T(8,128)(2,1)} %fusion.69) | data formatting | bytes 8388608 | tf_op jit(solution)/shard_map/while/body/eval_jaxpr/convert_element_type | solution.py:19
  334.5 10.6 %fusion.71 = bf16[32,256,256]{2,1,0:T(8,128)(2,1)} fusion(bf16[32,256,256]{1,2,0:T(8,128)(2,1)} %copy.28, bf16[4,32,256,256]{3,2,1,0:T(8,128)(2,1)} %get-tuple-element.159, s32[]{:T(128)S(6)} %copy.32, f32[32]{0:T(128)S(1)} %get-tuple-element.133, f32[32]{0:T(128)S(1)} %get-tuple-element.132, bf16[32,256,256]{2,1,0:T(8,128)(2,1)} %fusion.70), kind=kOutput, calls=%fused_computation.8.clone.1 | convolution fusion | flops 2157969408 | bytes 20971780 | tf_op jit(solution)/shard_map/while/body/eval_jaxpr/sba,sbc->sac/dot_general | solution.py:36
  345.1 9.6 %broadcast_multiply_fusion.2 = f32[32,256,256]{2,1,0:T(8,128)} fusion(f32[32]{0:T(128)S(1)} %get-tuple-element.132, bf16[32,256,256]{2,0,1:T(8,128)(2,1)} %copy-done, bf16[32,256,256]{2,1,0:T(8,128)(2,1)} %fusion.71), kind=kOutput, calls=%fused_computation.18.clone.1 | convolution fusion | flops 1075838976 | bytes 16777344 | tf_op jit(solution)/shard_map/while/body/eval_jaxpr/sab,sbc->sac/dot_general | solution.py:39
  354.7 18.8 %scatter_fusion = f32[96,256,256]{2,1,0:T(8,128)} fusion(f32[96,256,256]{2,1,0:T(8,128)} %get-tuple-element.144, s32[32]{0:T(128)S(1)} %fusion.66, f32[32,256,256]{2,1,0:T(8,128)} %broadcast_multiply_fusion.2), kind=kCustom, calls=%fused_computation.1.clone.1 | custom fusion | flops 2097152 | bytes 25165952 | tf_op jit(solution)/shard_map/while/body/eval_jaxpr/scatter-add | solution.py:71
  373.5 13.2 %convert_element_type.64 = bf16[96,256,256]{2,1,0:T(8,128)(2,1)} convert(f32[96,256,256]{2,1,0:T(8,128)} %get-tuple-element.44) | non-fusion elementwise | flops 6291456 | bytes 37748736 | tf_op jit(solution)/shard_map/convert_element_type | solution.py:77
  386.7 94.3 %reduce-scatter.4.cloned.1.call-done = bf16[1,1,6,256,256]{4,3,2,1,0:T(8,128)(2,1)} async-done(((bf16[16,1,6,256,256]{4,3,2,1,0:T(8,128)(2,1)}), bf16[1,1,6,256,256]{4,3,2,1,0:T(8,128)(2,1)}) %reduce-scatter.4.cloned.1.call-update) | async-done | bytes 786448
  484.2 64.5 %psum.7 = f32[]{:T(128)} all-reduce(f32[]{:T(128)} %get-tuple-element.79), channel_id=1, replica_groups=mesh['patch'=16,'exp'=8] {'patch','exp'}, use_global_device_ids=true, to_apply=%region_5.6 | all-reduce | flops 1 | bytes 8 | tf_op jit(solution)/shard_map/psum | solution.py:84
  (60 shorter events, 24.4 us)
Async XLA Ops:
  7.2 96.9 %all-gather.2.cloned.1.call-start = ((), (), s32[]{:S(2)}) async-start(), calls=%async_computation.1 | async-start | bytes 13369344 | tf_op jit(solution)/shard_map/all_gather | solution.py:54
  9.6 471.4 %reduce-scatter.4.cloned.1.call-start = ((), (), s32[]{:S(2)}) async-start(), calls=%async_computation.2 | async-start | bytes 13369344
  123.0 2.2 copy-start.1
  125.2 5.0 copy-start
  187.5 2.2 copy-start.1
  189.7 5.0 copy-start
  252.0 2.2 copy-start.1
  254.2 5.0 copy-start
  316.5 2.2 copy-start.1
  318.7 5.0 copy-start
  386.7 94.3 %copy-start.2 = (f32[1,1,6,256,256]{4,3,2,1,0:T(8,128)S(1)}, f32[1,1,6,256,256]{4,3,2,1,0:T(8,128)}, u32[]{:S(2)}) copy-start(f32[1,1,6,256,256]{4,3,2,1,0:T(8,128)} %param.9) | copy-start | bytes 4718596
Sparse Core Ops, SparseCore 0:
  10.7 93.3 all-gather.1
  386.8 94.1 reduce-scatter.3
where the time goes:
time: 559 us; the launch traced here: 557 us
  waiting for transfers between devices  186 us (33%)
  matrix products  119 us (21%)
  other arithmetic  94.9 us (17%)
  local copies, waits for them, and re-layouts  77 us (14%)
  blocking collectives  64.5 us (12%)
  between operations  15.9 us (3%)
    unnamed x3, waiting for transfers between devices  94.3 us
    all_gather x1, waiting for transfers between devices, per_device(): gathered = lax.all_gather(model_half, 'patch', axis=0, tiled=True)  91.4 us
    scatter-add x4, other arithmetic, source_block(): return (running.at[keys_block].add(adjoint), None)  75.2 us
    psum x1, blocking collectives, per_device(): square_sum = lax.psum(jnp.sum(step_field * step_field), ('patch', 'exp'))  64.5 us
    dot_general x4, matrix products, stamp_adjoint(): jnp.einsum('sba,sbc->sac', row_kernel, residual, preferred_element_type=j...  42.6 us
    dot_general x4, matrix products, stamp_adjoint(): jnp.einsum('sab,sbc->sac', backward, col_kernel, preferred_element_type=j...  38.3 us
    convert_element_type x4, local copies, waits for them, and re-layouts, banded_matrices(): return jnp.einsum('sk,kij->sij', tap_values, tap_table, preferred_element...  30.1 us
    gather x4, local copies, waits for them, and re-layouts, source_block(): tile_sel = jnp.take(flat_tiles, keys_block, axis=0)  29.4 us
  transfers between devices with their start and end apart: 2, of which 2 were waited for; matrix products, arithmetic and copies ran while one was open for 1% of the time, Pallas kernels for 0%

commit v1 on v0

--- a/solution.py
+++ b/solution.py
@@ -4,6 +4,27 @@
 from jax.sharding import PartitionSpec as P
 
 step_rate = 0.2
+
+
+def collect(x, axis, dim):
+    devices, index, width = (lax.axis_size(axis), lax.axis_index(axis), x.shape[dim])
+    ahead = [(i, (i + 1) % devices) for i in range(devices)]
+    left = [(i, (i - 1) % devices) for i in range(devices)]
+    whole = jnp.zeros((*x.shape[:dim], devices * width, *x.shape[dim + 1 :]), x.dtype)
+    whole = lax.dynamic_update_slice_in_dim(whole, x, index * width, axis=dim)
+    from_left = from_right = x
+    half = devices // 2
+    for step in range(1, half + 1):
+        from_left = lax.ppermute(from_left, axis, ahead)
+        whole = lax.dynamic_update_slice_in_dim(
+            whole, from_left, (index - step) % devices * width, axis=dim
+        )
+        if step < devices - half:
+            from_right = lax.ppermute(from_right, axis, left)
+            whole = lax.dynamic_update_slice_in_dim(
+                whole, from_right, (index + step) % devices * width, axis=dim
+            )
+    return whole
 
 
 def banded_matrices(tap_values, tile_size):
@@ -51,7 +72,7 @@
     block_rows = 32
     model_half = sky_model.astype(jnp.bfloat16)
     patches = lax.axis_size("patch")
-    gathered = lax.all_gather(model_half, "patch", axis=0, tiled=True)
+    gathered = collect(model_half, "patch", 0)
     key_count = gathered.shape[0] * band_count
     flat_tiles = gathered.reshape(key_count, tile_size, tile_size)
     tile_keys = stamp_patch[:, 0] * band_count + stamp_band

time: 559 us -> 640 us (1.14)
  starting transfers between devices: 0.08 us -> 36.4 us
  local copies, waits for them, and re-layouts: 77 us -> 103 us
  waiting for transfers between devices: 186 us -> 197 us
  matrix products: 119 us -> 129 us
    ppermute x0 -> x15, waiting for transfers between devices: none -> 99.1 us  [the longest x8 99 us: collect(): from_left = lax.ppermute(from_left, axis, ahead)]
    all_gather x1 -> x0, waiting for transfers between devices: 91.4 us -> none  [per_device(): gathered = lax.all_gather(model_half, 'patch', axis=0, tiled=True)]
    ppermute x0 -> x15, starting transfers between devices: none -> 36.4 us  [the longest x7 34.4 us: collect(): from_right = lax.ppermute(from_right, axis, left)]
    dynamic_update_slice x0 -> x15, local copies, waits for them, and re-layouts: none -> 17.7 us  [the longest x7 8.88 us: collect(): lax.dynamic_update_slice_in_dim(whole, from_right, (index + step) % devic...]
    dot_general x4, matrix products: 19.8 us -> 29.1 us  [stamp_adjoint(): jnp.einsum('sab,scb->sac', tile_sel, col_kernel, preferred_element_type=j...]
    unnamed x3 -> x2, waiting for transfers between devices: 94.3 us -> 97.9 us
  transfers between devices with their start and end apart: 2 -> 16, of which waited for: 2 -> 10; matrix products, arithmetic and copies ran while one was open for 1% -> 3% of each run, Pallas kernels for 0% -> 0%
where the time goes in v1:
time: 640 us; the launch traced here: 639 us
  waiting for transfers between devices  197 us (31%)
  matrix products  129 us (20%)
  local copies, waits for them, and re-layouts  103 us (16%)
  other arithmetic  92.8 us (14%)
  blocking collectives  64.5 us (10%)
  starting transfers between devices  36.4 us (6%)
  between operations  16.3 us (3%)
    ppermute x8, waiting for transfers between devices, collect(): from_left = lax.ppermute(from_left, axis, ahead)  99 us
    unnamed x2, waiting for transfers between devices  97.9 us
    scatter-add x4, other arithmetic, source_block(): return (running.at[keys_block].add(adjoint), None)  75.1 us
    psum x1, blocking collectives, per_device(): square_sum = lax.psum(jnp.sum(step_field * step_field), ('patch', 'exp'))  64.5 us
    dot_general x4, matrix products, stamp_adjoint(): jnp.einsum('sba,sbc->sac', row_kernel, residual, preferred_element_type=j...  42.7 us
    dot_general x4, matrix products, stamp_adjoint(): jnp.einsum('sab,sbc->sac', backward, col_kernel, preferred_element_type=j...  38.2 us
    ppermute x7, starting transfers between devices, collect(): from_right = lax.ppermute(from_right, axis, left)  34.4 us
    convert_element_type x4, local copies, waits for them, and re-layouts, banded_matrices(): return jnp.einsum('sk,kij->sij', tap_values, tap_table, preferred_element...  30.1 us
  transfers between devices with their start and end apart: 16, of which 10 were waited for; matrix products, arithmetic and copies ran while one was open for 3% of the time, Pallas kernels for 0%

profile of v1, /device:TPU:1, one launch (start us, length us, event | category | flops | bytes accessed | tf_op | source)
XLA Modules:
  0.0 638.5 jit_solution(4541590642013156706)
XLA Ops:
  21.2 17.3 %collective-permute-done = bf16[1,1,6,256,256]{4,3,2,1,0:T(8,128)(2,1)S(1)} collective-permute-done((bf16[1,1,6,256,256]{4,3,2,1,0:T(8,128)(2,1)S(1)}, bf16[1,1,6,256,256]{4,3,2,1,0:T(8,128)(2,1)S(1)}, u32[]{:S(2)}, u32[]{:S(2)}) %collective-permute-start) | collective-permute-done | bytes 786464 | tf_op jit(solution)/shard_map/ppermute | solution.py:18
  43.3 16.3 %collective-permute-done.2 = bf16[1,1,6,256,256]{4,3,2,1,0:T(8,128)(2,1)S(1)} collective-permute-done((bf16[1,1,6,256,256]{4,3,2,1,0:T(8,128)(2,1)S(1)}, bf16[1,1,6,256,256]{4,3,2,1,0:T(8,128)(2,1)S(1)}, u32[]{:S(2)}, u32[]{:S(2)}) %collective-permute-start.2) | collective-permute-done | bytes 786464 | tf_op jit(solution)/shard_map/ppermute | solution.py:18
  64.4 15.4 %collective-permute-done.4 = bf16[1,1,6,256,256]{4,3,2,1,0:T(8,128)(2,1)S(1)} collective-permute-done((bf16[1,1,6,256,256]{4,3,2,1,0:T(8,128)(2,1)S(1)}, bf16[1,1,6,256,256]{4,3,2,1,0:T(8,128)(2,1)S(1)}, u32[]{:S(2)}, u32[]{:S(2)}) %collective-permute-start.4) | collective-permute-done | bytes 786464 | tf_op jit(solution)/shard_map/ppermute | solution.py:18
  89.2 9.9 %collective-permute-done.6 = bf16[1,1,6,256,256]{4,3,2,1,0:T(8,128)(2,1)S(1)} collective-permute-done((bf16[1,1,6,256,256]{4,3,2,1,0:T(8,128)(2,1)S(1)}, bf16[1,1,6,256,256]{4,3,2,1,0:T(8,128)(2,1)S(1)}, u32[]{:S(2)}, u32[]{:S(2)}) %collective-permute-start.6) | collective-permute-done | bytes 786464 | tf_op jit(solution)/shard_map/ppermute | solution.py:18
  107.8 9.6 %collective-permute-done.8 = bf16[1,1,6,256,256]{4,3,2,1,0:T(8,128)(2,1)S(1)} collective-permute-done((bf16[1,1,6,256,256]{4,3,2,1,0:T(8,128)(2,1)S(1)}, bf16[1,1,6,256,256]{4,3,2,1,0:T(8,128)(2,1)S(1)}, u32[]{:S(2)}, u32[]{:S(2)}) %collective-permute-start.8) | collective-permute-done | bytes 786464 | tf_op jit(solution)/shard_map/ppermute | solution.py:18
  125.9 9.0 %collective-permute-done.10 = bf16[1,1,6,256,256]{4,3,2,1,0:T(8,128)(2,1)S(1)} collective-permute-done((bf16[1,1,6,256,256]{4,3,2,1,0:T(8,128)(2,1)S(1)}, bf16[1,1,6,256,256]{4,3,2,1,0:T(8,128)(2,1)S(1)}, u32[]{:S(2)}, u32[]{:S(2)}) %collective-permute-start.10) | collective-permute-done | bytes 786464 | tf_op jit(solution)/shard_map/ppermute | solution.py:18
  143.1 8.3 %collective-permute-done.12 = bf16[1,1,6,256,256]{4,3,2,1,0:T(8,128)(2,1)S(1)} collective-permute-done((bf16[1,1,6,256,256]{4,3,2,1,0:T(8,128)(2,1)S(1)}, bf16[1,1,6,256,256]{4,3,2,1,0:T(8,128)(2,1)S(1)}, u32[]{:S(2)}, u32[]{:S(2)}) %collective-permute-start.12) | collective-permute-done | bytes 786464 | tf_op jit(solution)/shard_map/ppermute | solution.py:18
  154.3 13.2 %collective-permute-done.14 = bf16[1,1,6,256,256]{4,3,2,1,0:T(8,128)(2,1)S(1)} collective-permute-done((bf16[1,1,6,256,256]{4,3,2,1,0:T(8,128)(2,1)S(1)}, bf16[1,1,6,256,256]{4,3,2,1,0:T(8,128)(2,1)S(1)}, u32[]{:S(2)}, u32[]{:S(2)}) %collective-permute-start.14) | collective-permute-done | bytes 786464 | tf_op jit(solution)/shard_map/ppermute | solution.py:18
  168.4 11.4 %broadcast_in_dim.14 = f32[96,256,256]{2,1,0:T(8,128)} broadcast(f32[]{:T(128)} %constant.129.clone.1), dimensions={} | broadcast | bytes 25165828 | tf_op jit(solution)/shard_map/broadcast_in_dim | solution.py:95
  179.8 271.2 %while.10 = (s32[]{:T(128)}, f32[96,256,256]{2,1,0:T(8,128)}, s32[4,32]{1,0:T(4,128)S(1)}, bf16[4,32]{1,0:T(4,128)(2,1)S(1)}, bf16[4,32,2,21]{1,3,2,0:T(8,128)(2...) while((s32[]{:T(128)}, f32[96,256,256]{2,1,0:T(8,128)}, ...), condition=%wide.region_2.3_spmd, body=%wide.region_0.2_spmd.sunk | while | flops 4494984704 | bytes 118250448 | solution.py:94
  179.9 7.3 %gather_fusion = bf16[32,256,256]{2,1,0:T(8,128)(2,1)} fusion(bf16[96,256,256]{2,1,0:T(8,128)(2,1)} %get-tuple-element.160, s32[1024]{0:T(1024)S(1)} %pad_clamp_fusion.2), kind=kCustom, calls=%fused_computation.clone.1 | custom fusion | bytes 8388736 | tf_op jit(solution)/shard_map/while/body/eval_jaxpr/jit(_take)/gather | solution.py:90
  201.1 7.5 %copy.76 = bf16[32,256,256]{1,2,0:T(8,128)(2,1)} copy(bf16[32,256,256]{2,0,1:T(8,128)(2,1)} %fusion.69) | data formatting | bytes 8388608 | tf_op jit(solution)/shard_map/while/body/eval_jaxpr/convert_element_type | solution.py:40
  208.7 10.7 %fusion.71 = bf16[32,256,256]{2,1,0:T(8,128)(2,1)} fusion(bf16[32,256,256]{1,2,0:T(8,128)(2,1)} %copy.76, bf16[4,32,256,256]{3,2,1,0:T(8,128)(2,1)} %get-tuple-element.161, s32[]{:T(128)S(6)} %copy.96, f32[32]{0:T(128)S(1)} %get-tuple-element.135, f32[32]{0:T(128)S(1)} %get-tuple-element.134, bf16[32,256,256]{2,1,0:T(8,128)(2,1)} %fusion.70), kind=kOutput, calls=%fused_computation.8.clone.1 | convolution fusion | flops 2157969408 | bytes 20971780 | tf_op jit(solution)/shard_map/while/body/eval_jaxpr/sba,sbc->sac/dot_general | solution.py:57
  219.3 9.5 %broadcast_multiply_fusion.2 = f32[32,256,256]{2,1,0:T(8,128)} fusion(f32[32]{0:T(128)S(1)} %get-tuple-element.134, bf16[32,256,256]{2,0,1:T(8,128)(2,1)} %copy-done, bf16[32,256,256]{2,1,0:T(8,128)(2,1)} %fusion.71), kind=kOutput, calls=%fused_computation.18.clone.1 | convolution fusion | flops 1075838976 | bytes 16777344 | tf_op jit(solution)/shard_map/while/body/eval_jaxpr/sab,sbc->sac/dot_general | solution.py:60
  228.9 18.7 %scatter_fusion = f32[96,256,256]{2,1,0:T(8,128)} fusion(f32[96,256,256]{2,1,0:T(8,128)} %get-tuple-element.146, s32[32]{0:T(128)S(1)} %fusion.66, f32[32,256,256]{2,1,0:T(8,128)} %broadcast_multiply_fusion.2), kind=kCustom, calls=%fused_computation.1.clone.1 | custom fusion | flops 2097152 | bytes 25165952 | tf_op jit(solution)/shard_map/while/body/eval_jaxpr/scatter-add | solution.py:92
  247.7 7.3 %gather_fusion = bf16[32,256,256]{2,1,0:T(8,128)(2,1)} fusion(bf16[96,256,256]{2,1,0:T(8,128)(2,1)} %get-tuple-element.160, s32[1024]{0:T(1024)S(1)} %pad_clamp_fusion.2), kind=kCustom, calls=%fused_computation.clone.1 | custom fusion | bytes 8388736 | tf_op jit(solution)/shard_map/while/body/eval_jaxpr/jit(_take)/gather | solution.py:90
  268.9 7.5 %copy.76 = bf16[32,256,256]{1,2,0:T(8,128)(2,1)} copy(bf16[32,256,256]{2,0,1:T(8,128)(2,1)} %fusion.69) | data formatting | bytes 8388608 | tf_op jit(solution)/shard_map/while/body/eval_jaxpr/convert_element_type | solution.py:40
  276.4 10.7 %fusion.71 = bf16[32,256,256]{2,1,0:T(8,128)(2,1)} fusion(bf16[32,256,256]{1,2,0:T(8,128)(2,1)} %copy.76, bf16[4,32,256,256]{3,2,1,0:T(8,128)(2,1)} %get-tuple-element.161, s32[]{:T(128)S(6)} %copy.96, f32[32]{0:T(128)S(1)} %get-tuple-element.135, f32[32]{0:T(128)S(1)} %get-tuple-element.134, bf16[32,256,256]{2,1,0:T(8,128)(2,1)} %fusion.70), kind=kOutput, calls=%fused_computation.8.clone.1 | convolution fusion | flops 2157969408 | bytes 20971780 | tf_op jit(solution)/shard_map/while/body/eval_jaxpr/sba,sbc->sac/dot_general | solution.py:57
  287.1 9.5 %broadcast_multiply_fusion.2 = f32[32,256,256]{2,1,0:T(8,128)} fusion(f32[32]{0:T(128)S(1)} %get-tuple-element.134, bf16[32,256,256]{2,0,1:T(8,128)(2,1)} %copy-done, bf16[32,256,256]{2,1,0:T(8,128)(2,1)} %fusion.71), kind=kOutput, calls=%fused_computation.18.clone.1 | convolution fusion | flops 1075838976 | bytes 16777344 | tf_op jit(solution)/shard_map/while/body/eval_jaxpr/sab,sbc->sac/dot_general | solution.py:60
  296.6 18.7 %scatter_fusion = f32[96,256,256]{2,1,0:T(8,128)} fusion(f32[96,256,256]{2,1,0:T(8,128)} %get-tuple-element.146, s32[32]{0:T(128)S(1)} %fusion.66, f32[32,256,256]{2,1,0:T(8,128)} %broadcast_multiply_fusion.2), kind=kCustom, calls=%fused_computation.1.clone.1 | custom fusion | flops 2097152 | bytes 25165952 | tf_op jit(solution)/shard_map/while/body/eval_jaxpr/scatter-add | solution.py:92
  315.4 7.3 %gather_fusion = bf16[32,256,256]{2,1,0:T(8,128)(2,1)} fusion(bf16[96,256,256]{2,1,0:T(8,128)(2,1)} %get-tuple-element.160, s32[1024]{0:T(1024)S(1)} %pad_clamp_fusion.2), kind=kCustom, calls=%fused_computation.clone.1 | custom fusion | bytes 8388736 | tf_op jit(solution)/shard_map/while/body/eval_jaxpr/jit(_take)/gather | solution.py:90
  336.6 7.5 %copy.76 = bf16[32,256,256]{1,2,0:T(8,128)(2,1)} copy(bf16[32,256,256]{2,0,1:T(8,128)(2,1)} %fusion.69) | data formatting | bytes 8388608 | tf_op jit(solution)/shard_map/while/body/eval_jaxpr/convert_element_type | solution.py:40
  344.2 10.7 %fusion.71 = bf16[32,256,256]{2,1,0:T(8,128)(2,1)} fusion(bf16[32,256,256]{1,2,0:T(8,128)(2,1)} %copy.76, bf16[4,32,256,256]{3,2,1,0:T(8,128)(2,1)} %get-tuple-element.161, s32[]{:T(128)S(6)} %copy.96, f32[32]{0:T(128)S(1)} %get-tuple-element.135, f32[32]{0:T(128)S(1)} %get-tuple-element.134, bf16[32,256,256]{2,1,0:T(8,128)(2,1)} %fusion.70), kind=kOutput, calls=%fused_computation.8.clone.1 | convolution fusion | flops 2157969408 | bytes 20971780 | tf_op jit(solution)/shard_map/while/body/eval_jaxpr/sba,sbc->sac/dot_general | solution.py:57
  354.8 9.5 %broadcast_multiply_fusion.2 = f32[32,256,256]{2,1,0:T(8,128)} fusion(f32[32]{0:T(128)S(1)} %get-tuple-element.134, bf16[32,256,256]{2,0,1:T(8,128)(2,1)} %copy-done, bf16[32,256,256]{2,1,0:T(8,128)(2,1)} %fusion.71), kind=kOutput, calls=%fused_computation.18.clone.1 | convolution fusion | flops 1075838976 | bytes 16777344 | tf_op jit(solution)/shard_map/while/body/eval_jaxpr/sab,sbc->sac/dot_general | solution.py:60
  364.4 18.8 %scatter_fusion = f32[96,256,256]{2,1,0:T(8,128)} fusion(f32[96,256,256]{2,1,0:T(8,128)} %get-tuple-element.146, s32[32]{0:T(128)S(1)} %fusion.66, f32[32,256,256]{2,1,0:T(8,128)} %broadcast_multiply_fusion.2), kind=kCustom, calls=%fused_computation.1.clone.1 | custom fusion | flops 2097152 | bytes 25165952 | tf_op jit(solution)/shard_map/while/body/eval_jaxpr/scatter-add | solution.py:92
  404.5 7.5 %copy.76 = bf16[32,256,256]{1,2,0:T(8,128)(2,1)} copy(bf16[32,256,256]{2,0,1:T(8,128)(2,1)} %fusion.69) | data formatting | bytes 8388608 | tf_op jit(solution)/shard_map/while/body/eval_jaxpr/convert_element_type | solution.py:40
  412.1 10.7 %fusion.71 = bf16[32,256,256]{2,1,0:T(8,128)(2,1)} fusion(bf16[32,256,256]{1,2,0:T(8,128)(2,1)} %copy.76, bf16[4,32,256,256]{3,2,1,0:T(8,128)(2,1)} %get-tuple-element.161, s32[]{:T(128)S(6)} %copy.96, f32[32]{0:T(128)S(1)} %get-tuple-element.135, f32[32]{0:T(128)S(1)} %get-tuple-element.134, bf16[32,256,256]{2,1,0:T(8,128)(2,1)} %fusion.70), kind=kOutput, calls=%fused_computation.8.clone.1 | convolution fusion | flops 2157969408 | bytes 20971780 | tf_op jit(solution)/shard_map/while/body/eval_jaxpr/sba,sbc->sac/dot_general | solution.py:57
  422.7 9.5 %broadcast_multiply_fusion.2 = f32[32,256,256]{2,1,0:T(8,128)} fusion(f32[32]{0:T(128)S(1)} %get-tuple-element.134, bf16[32,256,256]{2,0,1:T(8,128)(2,1)} %copy-done, bf16[32,256,256]{2,1,0:T(8,128)(2,1)} %fusion.71), kind=kOutput, calls=%fused_computation.18.clone.1 | convolution fusion | flops 1075838976 | bytes 16777344 | tf_op jit(solution)/shard_map/while/body/eval_jaxpr/sab,sbc->sac/dot_general | solution.py:60
  432.3 18.8 %scatter_fusion = f32[96,256,256]{2,1,0:T(8,128)} fusion(f32[96,256,256]{2,1,0:T(8,128)} %get-tuple-element.146, s32[32]{0:T(128)S(1)} %fusion.66, f32[32,256,256]{2,1,0:T(8,128)} %broadcast_multiply_fusion.2), kind=kCustom, calls=%fused_computation.1.clone.1 | custom fusion | flops 2097152 | bytes 25165952 | tf_op jit(solution)/shard_map/while/body/eval_jaxpr/scatter-add | solution.py:92
  451.1 13.2 %convert_element_type.64 = bf16[96,256,256]{2,1,0:T(8,128)(2,1)} convert(f32[96,256,256]{2,1,0:T(8,128)} %get-tuple-element.44) | non-fusion elementwise | flops 6291456 | bytes 37748736 | tf_op jit(solution)/shard_map/convert_element_type | solution.py:98
  464.3 97.9 %reduce-scatter.4.cloned.1.call-done = bf16[1,1,6,256,256]{4,3,2,1,0:T(8,128)(2,1)} async-done(((bf16[16,1,6,256,256]{4,3,2,1,0:T(8,128)(2,1)}), bf16[1,1,6,256,256]{4,3,2,1,0:T(8,128)(2,1)}) %reduce-scatter.4.cloned.1.call-update) | async-done | bytes 786448
  565.4 64.5 %psum.7 = f32[]{:T(128)} all-reduce(f32[]{:T(128)} %get-tuple-element.81), channel_id=1, replica_groups=mesh['patch'=16,'exp'=8] {'patch','exp'}, use_global_device_ids=true, to_apply=%region_5.6 | all-reduce | flops 1 | bytes 8 | tf_op jit(solution)/shard_map/psum | solution.py:105
  (111 shorter events, 128.0 us)
Async XLA Ops:
  7.2 6.3 copy-start.1
  7.2 72.9 %copy-start.6 = (bf16[128]{0:T(256)(128)(2,1)S(1)}, bf16[128]{0:T(256)(128)(2,1)}, u32[]{:S(2)}) copy-start(bf16[128]{0:T(256)(128)(2,1)} %param.14) | copy-start | bytes 772
  7.2 73.0 %copy-start.7 = (bf16[128]{0:T(256)(128)(2,1)S(1)}, bf16[128]{0:T(256)(128)(2,1)}, u32[]{:S(2)}) copy-start(bf16[128]{0:T(256)(128)(2,1)} %param.15) | copy-start | bytes 772
  7.2 73.1 %copy-start.8 = (s32[128]{0:T(128)S(1)}, s32[128]{0:T(128)}, u32[]{:S(2)}) copy-start(s32[128]{0:T(128)} %param.12) | copy-start | bytes 1540
  7.2 73.1 %copy-start.9 = (s32[128,1]{0,1:T(1,128)S(1)}, s32[128,1]{0,1:T(1,128)}, u32[]{:S(2)}) copy-start(s32[128,1]{0,1:T(1,128)} %param.11) | copy-start | bytes 1540
  7.2 73.2 %copy-start.5 = (bf16[128,2,21]{0,1,2:T(2,128)(2,1)S(1)}, bf16[128,2,21]{0,1,2:T(2,128)(2,1)}, u32[]{:S(2)}) copy-start(bf16[128,2,21]{0,1,2:T(2,128)(2,1)} %param.13) | copy-start | bytes 32260
  7.2 554.9 %reduce-scatter.4.cloned.1.call-start = ((), (), s32[]{:S(2)}) async-start(), calls=%async_computation.1 | async-start | bytes 13369344
  14.5 24.0 %collective-permute-start = (bf16[1,1,6,256,256]{4,3,2,1,0:T(8,128)(2,1)S(1)}, bf16[1,1,6,256,256]{4,3,2,1,0:T(8,128)(2,1)S(1)}, u32[]{:S(2)}, u32[]{:S(2)}) collective-permute-start(bf16[1,1,6,256,256]{4,3,2,1,0:T(8,128)(2,1)S(1)} %get-tuple-element.78), channel_id=1, source_target_pairs={{0,8},{8,16},{16,24},{24,32},{32,40},{40,48},{48,56},{56,64},{64,7... | collective-permute-start | bytes 2359304 | tf_op jit(solution)/shard_map/ppermute | solution.py:18
  16.5 22.0 %collective-permute-start.1 = (bf16[1,1,6,256,256]{4,3,2,1,0:T(8,128)(2,1)S(1)}, bf16[1,1,6,256,256]{4,3,2,1,0:T(8,128)(2,1)S(1)}, u32[]{:S(2)}, u32[]{:S(2)}) collective-permute-start(bf16[1,1,6,256,256]{4,3,2,1,0:T(8,128)(2,1)S(1)} %get-tuple-element.78), channel_id=1, source_target_pairs={{0,120},{8,0},{16,8},{24,16},{32,24},{40,32},{48,40},{56,48},{64,5... | collective-permute-start | bytes 2359304 | tf_op jit(solution)/shard_map/ppermute | solution.py:23
  38.5 41.3 %copy-start.4 = (bf16[1,1,6,256,256]{4,3,2,1,0:T(8,128)(2,1)}, bf16[1,1,6,256,256]{4,3,2,1,0:T(8,128)(2,1)S(1)}, u32[]{:S(2)}) copy-start(bf16[1,1,6,256,256]{4,3,2,1,0:T(8,128)(2,1)S(1)} %collective-permute-done) | copy-start | bytes 2359300
  38.5 21.1 %collective-permute-start.2 = (bf16[1,1,6,256,256]{4,3,2,1,0:T(8,128)(2,1)S(1)}, bf16[1,1,6,256,256]{4,3,2,1,0:T(8,128)(2,1)S(1)}, u32[]{:S(2)}, u32[]{:S(2)}) collective-permute-start(bf16[1,1,6,256,256]{4,3,2,1,0:T(8,128)(2,1)S(1)} %collective-permute-done), channel_id=1, source_target_pairs={{0,8},{8,16},{16,24},{24,32},{32,40},{40,48},{48,56},{56,64},{64,7... | collective-permute-start | bytes 2359304 | tf_op jit(solution)/shard_map/ppermute | solution.py:18
  38.5 41.3 %copy-start.3 = (bf16[1,1,6,256,256]{4,3,2,1,0:T(8,128)(2,1)}, bf16[1,1,6,256,256]{4,3,2,1,0:T(8,128)(2,1)S(1)}, u32[]{:S(2)}) copy-start(bf16[1,1,6,256,256]{4,3,2,1,0:T(8,128)(2,1)S(1)} %collective-permute-done.1) | copy-start | bytes 2359300
  38.5 21.1 %collective-permute-start.3 = (bf16[1,1,6,256,256]{4,3,2,1,0:T(8,128)(2,1)S(1)}, bf16[1,1,6,256,256]{4,3,2,1,0:T(8,128)(2,1)}, u32[]{:S(2)}, u32[]{:S(2)}) collective-permute-start(bf16[1,1,6,256,256]{4,3,2,1,0:T(8,128)(2,1)S(1)} %collective-permute-done.1), channel_id=1, source_target_pairs={{0,120},{8,0},{16,8},{24,16},{32,24},{40,32},{48,40},{56,48},{64,5... | collective-permute-start | bytes 2359304 | tf_op jit(solution)/shard_map/ppermute | solution.py:23
  59.6 20.2 %collective-permute-start.4 = (bf16[1,1,6,256,256]{4,3,2,1,0:T(8,128)(2,1)S(1)}, bf16[1,1,6,256,256]{4,3,2,1,0:T(8,128)(2,1)S(1)}, u32[]{:S(2)}, u32[]{:S(2)}) collective-permute-start(bf16[1,1,6,256,256]{4,3,2,1,0:T(8,128)(2,1)S(1)} %collective-permute-done.2), channel_id=1, source_target_pairs={{0,8},{8,16},{16,24},{24,32},{32,40},{40,48},{48,56},{56,64},{64,7... | collective-permute-start | bytes 2359304 | tf_op jit(solution)/shard_map/ppermute | solution.py:18
  59.6 23.0 %collective-permute-start.5 = (bf16[1,1,6,256,256]{4,3,2,1,0:T(8,128)(2,1)}, bf16[1,1,6,256,256]{4,3,2,1,0:T(8,128)(2,1)S(1)}, u32[]{:S(2)}, u32[]{:S(2)}) collective-permute-start(bf16[1,1,6,256,256]{4,3,2,1,0:T(8,128)(2,1)} %collective-permute-done.3), channel_id=1, source_target_pairs={{0,120},{8,0},{16,8},{24,16},{32,24},{40,32},{48,40},{56,48},{64,5... | collective-permute-start | bytes 2359304 | tf_op jit(solution)/shard_map/ppermute | solution.py:23
  79.8 19.3 %collective-permute-start.6 = (bf16[1,1,6,256,256]{4,3,2,1,0:T(8,128)(2,1)S(1)}, bf16[1,1,6,256,256]{4,3,2,1,0:T(8,128)(2,1)S(1)}, u32[]{:S(2)}, u32[]{:S(2)}) collective-permute-start(bf16[1,1,6,256,256]{4,3,2,1,0:T(8,128)(2,1)S(1)} %collective-permute-done.4), channel_id=1, source_target_pairs={{0,8},{8,16},{16,24},{24,32},{32,40},{40,48},{48,56},{56,64},{64,7... | collective-permute-start | bytes 2359304 | tf_op jit(solution)/shard_map/ppermute | solution.py:18
  82.7 19.5 %collective-permute-start.7 = (bf16[1,1,6,256,256]{4,3,2,1,0:T(8,128)(2,1)S(1)}, bf16[1,1,6,256,256]{4,3,2,1,0:T(8,128)(2,1)S(1)}, u32[]{:S(2)}, u32[]{:S(2)}) collective-permute-start(bf16[1,1,6,256,256]{4,3,2,1,0:T(8,128)(2,1)S(1)} %collective-permute-done.5), channel_id=1, source_target_pairs={{0,120},{8,0},{16,8},{24,16},{32,24},{40,32},{48,40},{56,48},{64,5... | collective-permute-start | bytes 2359304 | tf_op jit(solution)/shard_map/ppermute | solution.py:23
  99.1 18.4 %collective-permute-start.8 = (bf16[1,1,6,256,256]{4,3,2,1,0:T(8,128)(2,1)S(1)}, bf16[1,1,6,256,256]{4,3,2,1,0:T(8,128)(2,1)S(1)}, u32[]{:S(2)}, u32[]{:S(2)}) collective-permute-start(bf16[1,1,6,256,256]{4,3,2,1,0:T(8,128)(2,1)S(1)} %collective-permute-done.6), channel_id=1, source_target_pairs={{0,8},{8,16},{16,24},{24,32},{32,40},{40,48},{48,56},{56,64},{64,7... | collective-permute-start | bytes 2359304 | tf_op jit(solution)/shard_map/ppermute | solution.py:18
  102.1 17.3 %collective-permute-start.9 = (bf16[1,1,6,256,256]{4,3,2,1,0:T(8,128)(2,1)S(1)}, bf16[1,1,6,256,256]{4,3,2,1,0:T(8,128)(2,1)S(1)}, u32[]{:S(2)}, u32[]{:S(2)}) collective-permute-start(bf16[1,1,6,256,256]{4,3,2,1,0:T(8,128)(2,1)S(1)} %collective-permute-done.7), channel_id=1, source_target_pairs={{0,120},{8,0},{16,8},{24,16},{32,24},{40,32},{48,40},{56,48},{64,5... | collective-permute-start | bytes 2359304 | tf_op jit(solution)/shard_map/ppermute | solution.py:23
  117.5 17.4 %collective-permute-start.10 = (bf16[1,1,6,256,256]{4,3,2,1,0:T(8,128)(2,1)S(1)}, bf16[1,1,6,256,256]{4,3,2,1,0:T(8,128)(2,1)S(1)}, u32[]{:S(2)}, u32[]{:S(2)}) collective-permute-start(bf16[1,1,6,256,256]{4,3,2,1,0:T(8,128)(2,1)S(1)} %collective-permute-done.8), channel_id=1, source_target_pairs={{0,8},{8,16},{16,24},{24,32},{32,40},{40,48},{48,56},{56,64},{64,7... | collective-permute-start | bytes 2359304 | tf_op jit(solution)/shard_map/ppermute | solution.py:18
  119.5 17.4 %collective-permute-start.11 = (bf16[1,1,6,256,256]{4,3,2,1,0:T(8,128)(2,1)S(1)}, bf16[1,1,6,256,256]{4,3,2,1,0:T(8,128)(2,1)S(1)}, u32[]{:S(2)}, u32[]{:S(2)}) collective-permute-start(bf16[1,1,6,256,256]{4,3,2,1,0:T(8,128)(2,1)S(1)} %collective-permute-done.9), channel_id=1, source_target_pairs={{0,120},{8,0},{16,8},{24,16},{32,24},{40,32},{48,40},{56,48},{64,5... | collective-permute-start | bytes 2359304 | tf_op jit(solution)/shard_map/ppermute | solution.py:23
  134.9 16.5 %collective-permute-start.12 = (bf16[1,1,6,256,256]{4,3,2,1,0:T(8,128)(2,1)S(1)}, bf16[1,1,6,256,256]{4,3,2,1,0:T(8,128)(2,1)S(1)}, u32[]{:S(2)}, u32[]{:S(2)}) collective-permute-start(bf16[1,1,6,256,256]{4,3,2,1,0:T(8,128)(2,1)S(1)} %collective-permute-done.10), channel_id=1, source_target_pairs={{0,8},{8,16},{16,24},{24,32},{32,40},{40,48},{48,56},{56,64},{64,7... | collective-permute-start | bytes 2359304 | tf_op jit(solution)/shard_map/ppermute | solution.py:18
  136.9 16.4 %collective-permute-start.13 = (bf16[1,1,6,256,256]{4,3,2,1,0:T(8,128)(2,1)S(1)}, bf16[1,1,6,256,256]{4,3,2,1,0:T(8,128)(2,1)S(1)}, u32[]{:S(2)}, u32[]{:S(2)}) collective-permute-start(bf16[1,1,6,256,256]{4,3,2,1,0:T(8,128)(2,1)S(1)} %collective-permute-done.11), channel_id=1, source_target_pairs={{0,120},{8,0},{16,8},{24,16},{32,24},{40,32},{48,40},{56,48},{64,5... | collective-permute-start | bytes 2359304 | tf_op jit(solution)/shard_map/ppermute | solution.py:23
  151.4 16.0 %collective-permute-start.14 = (bf16[1,1,6,256,256]{4,3,2,1,0:T(8,128)(2,1)S(1)}, bf16[1,1,6,256,256]{4,3,2,1,0:T(8,128)(2,1)S(1)}, u32[]{:S(2)}, u32[]{:S(2)}) collective-permute-start(bf16[1,1,6,256,256]{4,3,2,1,0:T(8,128)(2,1)S(1)} %collective-permute-done.12), channel_id=1, source_target_pairs={{0,8},{8,16},{16,24},{24,32},{32,40},{40,48},{48,56},{56,64},{64,7... | collective-permute-start | bytes 2359304 | tf_op jit(solution)/shard_map/ppermute | solution.py:18
  188.6 1.9 copy-start
  256.3 1.9 copy-start
  324.1 1.9 copy-start
  391.9 1.9 copy-start
  464.3 97.9 %copy-start.2 = (f32[1,1,6,256,256]{4,3,2,1,0:T(8,128)S(1)}, f32[1,1,6,256,256]{4,3,2,1,0:T(8,128)}, u32[]{:S(2)}) copy-start(f32[1,1,6,256,256]{4,3,2,1,0:T(8,128)} %param.9) | copy-start | bytes 4718596
Sparse Core Ops, SparseCore 0:
  464.4 97.6 reduce-scatter.3
